TPU v7x, 32 devices: a whole 2x2x4 slice. The times are simulated.
32 devices in a mesh: dp: 2 (over x), pipe: 2 (over core), ctx: 8 (over z, y).
Axes of the slice: x: 2, y: 2, z: 4, core: 2. Of those that a mesh axis runs over, the one named last changes fastest.
Arguments:
- section_input: bfloat16 [2, 2, 1024, 2048], P('dp', 'pipe', 'ctx'), may hold values from -6 to 6
- section_positions: int32 [2, 2, 1024], P('dp', 'pipe', 'ctx'), may hold values from 0 to 1023, as said below
- saved_input: bfloat16 [2, 2, 1024, 2048], P('dp', 'pipe', 'ctx'), may hold values from -6 to 6
- saved_positions: int32 [2, 2, 1024], P('dp', 'pipe', 'ctx'), may hold values from 0 to 1023, as said below
- cotangent: bfloat16 [2, 2, 1024, 2048], P('dp', 'pipe', 'ctx'), may hold values from -6 to 6
- norm_gains: float32 [2, 2, 2, 2048], P(None, 'pipe'), may hold values from -2 to 2
- output_gains: float32 [2, 2, 2048], P(None, 'pipe'), may hold values from 0.25 to 2
- plan: int32 [2, 2, 2], P('dp', 'pipe'), may hold values from 0 to 1
Outputs:
- next_input: bfloat16 [2, 2, 1024, 2048], P('dp', 'pipe', 'ctx')
- upstream_grad: bfloat16 [2, 2, 1024, 2048], P('dp', 'pipe', 'ctx')
- gain_grads: float32 [2, 3, 2048], P('pipe')
Inputs may be any that keep to these rules, and one draw needn't show every extreme that they name: `section_positions`: in every sequence the first position is 0 and each later one is either one more than the position before it or 0 (a new document). `saved_positions`: in every sequence the first position is 0 and each later one is either one more than the position before it or 0 (a new document).
All inputs are finite; a program needn't handle non-finite values.
Results may differ from a plain program's by a relative error of at most 0.0075.
Values may be sent and summed in bfloat16 or wider, within the bound.
A program may use at most 64 MiB of HBM per device.

v0:
```python
import jax
import jax.numpy as jnp
from jax import lax
from jax.sharding import PartitionSpec as P

HEADS = 16
HEAD_DIM = 128
FEATURES = 2048
WINDOW = 512
TOK_DEV = 128
EPSILON = 1e-06


def passed_along(value, axis, steps):
    count = lax.axis_size(axis)
    first, last = (max(0, -steps), min(count, count - steps))
    return lax.ppermute(value, axis, [(source, source + steps) for source in range(first, last)])


def shifted(value, axis, steps):
    count = lax.axis_size(axis)
    pairs = [(source, (source + steps) % count) for source in range(count)]
    return lax.ppermute(value, axis, pairs)


def as_bfloat(values):
    narrow = lax.optimization_barrier(values.astype(jnp.bfloat16)).astype(jnp.float32)
    return values + lax.stop_gradient(narrow - values)


def attend(key_rows, key_pos, key_ok, gains, query_count):
    total_rows = key_rows.shape[0]
    first_row = total_rows - query_count
    shaped = key_rows.reshape(total_rows, HEADS, HEAD_DIM)
    normed = shaped * lax.rsqrt(jnp.mean(shaped * shaped, axis=-1, keepdims=True) + EPSILON)
    query_gain = gains[0].reshape(HEADS, HEAD_DIM)
    key_gain = gains[1].reshape(HEADS, HEAD_DIM)
    queries = as_bfloat(normed[first_row:] * query_gain)
    key_vecs = as_bfloat(normed * key_gain)
    scores = jnp.einsum("qhe,khe->hqk", queries, key_vecs) / jnp.sqrt(jnp.float32(HEAD_DIM))
    query_ids = first_row + jnp.arange(query_count, dtype=jnp.int32)
    key_ids = jnp.arange(total_rows, dtype=jnp.int32)
    distance = query_ids[:, None] - key_ids[None, :]
    query_pos = key_pos[first_row:]
    allowed = (
        (distance >= 0)
        & (distance < WINDOW)
        & (query_pos[:, None] - key_pos[None, :] == distance)
        & key_ok[None, :]
    )
    weights = jnp.where(allowed[None], jnp.exp(scores), jnp.float32(0.0))
    probability = as_bfloat(weights / jnp.sum(weights, axis=-1, keepdims=True))
    mixture = jnp.einsum("hqk,khe->qhe", probability, shaped)
    return key_rows[first_row:] + mixture.reshape(query_count, FEATURES) * gains[2]


def pick_gains(norm_gains, output_gains, lap_index):
    pair_gains = lax.dynamic_index_in_dim(norm_gains, lap_index, 0, keepdims=False)[0]
    out_gain = lax.dynamic_index_in_dim(output_gains, lap_index, 0, keepdims=False)[0]
    return jnp.concatenate([pair_gains, out_gain[None]], axis=0)


def local(
    section_input,
    section_positions,
    saved_input,
    saved_positions,
    cotangent,
    norm_gains,
    output_gains,
    plan,
):
    own_rows = section_input[0, 0]
    own_pos = section_positions[0, 0]
    saved_rows = saved_input[0, 0]
    saved_pos = saved_positions[0, 0]
    incoming = cotangent[0, 0]
    shard_rows = own_rows.shape[0]
    piece_len = min(WINDOW, shard_rows)
    piece_count = WINDOW // piece_len
    shard_index = lax.axis_index("ctx")
    pieces = (own_rows, own_pos, saved_rows, saved_pos)
    received = []
    for reach in range(1, piece_count + 1):
        received.append(passed_along((pieces[0], pieces[1], pieces[2], pieces[3]), "ctx", reach))
    ordered = received[::-1]
    ok_parts = [
        jnp.broadcast_to(shard_index >= reach, (piece_len,)) for reach in range(piece_count, 0, -1)
    ]
    key_ok = jnp.concatenate(ok_parts + [jnp.ones((shard_rows,), bool)])
    forward_gains = pick_gains(norm_gains, output_gains, plan[0, 0, 0])
    backward_gains = pick_gains(norm_gains, output_gains, plan[0, 0, 1])
    forward_keys = jnp.concatenate([piece[0] for piece in ordered] + [own_rows], axis=0).astype(
        jnp.float32
    )
    forward_pos = jnp.concatenate([piece[1] for piece in ordered] + [own_pos], axis=0)
    produced = attend(forward_keys, forward_pos, key_ok, forward_gains, shard_rows).astype(
        jnp.bfloat16
    )
    next_input = shifted(produced, "pipe", 1)
    saved_keys = jnp.concatenate([piece[2] for piece in ordered] + [saved_rows], axis=0).astype(
        jnp.float32
    )
    saved_key_pos = jnp.concatenate([piece[3] for piece in ordered] + [saved_pos], axis=0)

    def local_layer(rows, gains):
        return attend(rows, saved_key_pos, key_ok, gains, shard_rows)

    _, pullback = jax.vjp(local_layer, saved_keys, backward_gains)
    key_grads, gain_grads = pullback(incoming.astype(jnp.float32))
    own_grads = key_grads[WINDOW:]
    arriving = jnp.zeros((piece_len, FEATURES), jnp.float32)
    for reach in range(1, piece_count + 1):
        first = (piece_count - reach) * piece_len
        outgoing = key_grads[first : first + piece_len].astype(jnp.bfloat16)
        arriving = arriving + passed_along(outgoing, "ctx", -reach).astype(jnp.float32)
    own_grads = own_grads.at[shard_rows - piece_len :].add(arriving)
    upstream_grad = shifted(own_grads.astype(jnp.bfloat16), "pipe", -1)
    gain_total = lax.psum(gain_grads, ("dp", "ctx"))
    gain_total = gain_total / jnp.float32(TOK_DEV)
    return (next_input[None, None], upstream_grad[None, None], gain_total[None])


def solution(mesh):
    placed = (
        P("dp", "pipe", "ctx", None),
        P("dp", "pipe", "ctx"),
        P("dp", "pipe", "ctx", None),
        P("dp", "pipe", "ctx"),
        P("dp", "pipe", "ctx", None),
        P(None, "pipe", None, None),
        P(None, "pipe", None),
        P("dp", "pipe", None),
    )
    return jax.shard_map(
        local,
        mesh=mesh,
        in_specs=placed,
        out_specs=(
            P("dp", "pipe", "ctx", None),
            P("dp", "pipe", "ctx", None),
            P("pipe", None, None),
        ),
        check_vma=False,
    )
```

profile of v0, /device:TPU:0, one launch (start us, length us, event | category | flops | bytes accessed | tf_op | source)
XLA Modules:
  0.0 320.6 jit_solution(6539457708362573059)
XLA Ops:
  0.6 6.0 %collective-permute-start.13 = (bf16[128,2048]{1,0:T(8,128)(2,1)}, bf16[128,2048]{1,0:T(8,128)(2,1)S(1)}, u32[]{:S(2)}, u32[]{:S(2)}) collective-permute-start(bf16[128,2048]{1,0:T(8,128)(2,1)} %bitcast.86), channel_id=1, source_target_pairs={{0,4},{1,5},{2,6},{3,7},{8,12},{9,13},{10,14},{11,15},{16,20},{17,... | collective-permute-start | bytes 1572872 | tf_op jit(solution)/shard_map/ppermute | solution.py:17
  6.6 4.5 %collective-permute-start.14 = (bf16[128,2048]{1,0:T(8,128)(2,1)}, bf16[128,2048]{1,0:T(8,128)(2,1)S(1)}, u32[]{:S(2)}, u32[]{:S(2)}) collective-permute-start(bf16[128,2048]{1,0:T(8,128)(2,1)} %bitcast.87), channel_id=1, source_target_pairs={{0,3},{1,4},{2,5},{3,6},{4,7},{8,11},{9,12},{10,13},{11,14},{12,15... | collective-permute-start | bytes 1572872 | tf_op jit(solution)/shard_map/ppermute | solution.py:17
  12.4 3.9 %collective-permute-start.16 = (bf16[128,2048]{1,0:T(8,128)(2,1)}, bf16[128,2048]{1,0:T(8,128)(2,1)}, u32[]{:S(2)}, u32[]{:S(2)}) collective-permute-start(bf16[128,2048]{1,0:T(8,128)(2,1)} %bitcast.89), channel_id=1, source_target_pairs={{0,1},{1,2},{2,3},{3,4},{4,5},{5,6},{6,7},{8,9},{9,10},{10,11},{11... | collective-permute-start | bytes 1572872 | tf_op jit(solution)/shard_map/ppermute | solution.py:17
  26.1 2.1 copy.34
  32.1 8.5 %collective-permute-done.4 = s32[128]{0:T(128)S(1)} collective-permute-done((s32[128]{0:T(128)}, s32[128]{0:T(128)S(1)}, u32[]{:S(2)}, u32[]{:S(2)}) %collective-permute-start.4) | collective-permute-done | bytes 544 | tf_op jit(solution)/shard_map/ppermute | solution.py:17
  40.6 38.0 %collective-permute-start.5 = (s32[128]{0:T(128)}, s32[128]{0:T(128)S(1)}, u32[]{:S(2)}, u32[]{:S(2)}) collective-permute-start(s32[128]{0:T(128)} %bitcast.117), channel_id=1, source_target_pairs={{0,3},{1,4},{2,5},{3,6},{4,7},{8,11},{9,12},{10,13},{11,14},{12,15... | collective-permute-start | bytes 1544 | tf_op jit(solution)/shard_map/ppermute | solution.py:17
  82.7 6.2 %collective-permute-start.7 = (s32[128]{0:T(128)}, s32[128]{0:T(128)S(1)}, u32[]{:S(2)}, u32[]{:S(2)}) collective-permute-start(s32[128]{0:T(128)} %bitcast.119), channel_id=1, source_target_pairs={{0,1},{1,2},{2,3},{3,4},{4,5},{5,6},{6,7},{8,9},{9,10},{10,11},{11... | collective-permute-start | bytes 1544 | tf_op jit(solution)/shard_map/ppermute | solution.py:17
  90.4 6.8 %collective-permute-start.9 = (s32[128]{0:T(128)}, s32[128]{0:T(128)S(1)}, u32[]{:S(2)}, u32[]{:S(2)}) collective-permute-start(s32[128]{0:T(128)} %bitcast.111), channel_id=1, source_target_pairs={{0,4},{1,5},{2,6},{3,7},{8,12},{9,13},{10,14},{11,15},{16,20},{17,... | collective-permute-start | bytes 1544 | tf_op jit(solution)/shard_map/ppermute | solution.py:17
  98.6 4.1 %collective-permute-start.10 = (s32[128]{0:T(128)}, s32[128]{0:T(128)S(1)}, u32[]{:S(2)}, u32[]{:S(2)}) collective-permute-start(s32[128]{0:T(128)} %bitcast.112), channel_id=1, source_target_pairs={{0,3},{1,4},{2,5},{3,6},{4,7},{8,11},{9,12},{10,13},{11,14},{12,15... | collective-permute-start | bytes 1544 | tf_op jit(solution)/shard_map/ppermute | solution.py:17
  104.2 3.4 %collective-permute-start.11 = (s32[128]{0:T(128)}, s32[128]{0:T(128)S(1)}, u32[]{:S(2)}, u32[]{:S(2)}) collective-permute-start(s32[128]{0:T(128)} %bitcast.113), channel_id=1, source_target_pairs={{0,2},{1,3},{2,4},{3,5},{4,6},{5,7},{8,10},{9,11},{10,12},{11,13},... | collective-permute-start | bytes 1544 | tf_op jit(solution)/shard_map/ppermute | solution.py:17
  109.0 4.1 %collective-permute-start.12 = (s32[128]{0:T(128)}, s32[128]{0:T(128)S(1)}, u32[]{:S(2)}, u32[]{:S(2)}) collective-permute-start(s32[128]{0:T(128)} %bitcast.114), channel_id=1, source_target_pairs={{0,1},{1,2},{2,3},{3,4},{4,5},{5,6},{6,7},{8,9},{9,10},{10,11},{11... | collective-permute-start | bytes 1544 | tf_op jit(solution)/shard_map/ppermute | solution.py:17
  114.5 19.6 %collective-permute-start = (bf16[128,2048]{1,0:T(8,128)(2,1)}, bf16[128,2048]{1,0:T(8,128)(2,1)}, u32[]{:S(2)}, u32[]{:S(2)}) collective-permute-start(bf16[128,2048]{1,0:T(8,128)(2,1)} %bitcast), channel_id=1, source_target_pairs={{0,4},{1,5},{2,6},{3,7},{8,12},{9,13},{10,14},{11,15},{16,20},{17,... | collective-permute-start | bytes 1572872 | tf_op jit(solution)/shard_map/ppermute | solution.py:17
  135.8 2.1 collective-permute-start.1
  138.9 2.1 collective-permute-start.2
  142.0 3.3 %collective-permute-start.3 = (bf16[128,2048]{1,0:T(8,128)(2,1)}, bf16[128,2048]{1,0:T(8,128)(2,1)}, u32[]{:S(2)}, u32[]{:S(2)}) collective-permute-start(bf16[128,2048]{1,0:T(8,128)(2,1)} %bitcast), channel_id=1, source_target_pairs={{0,1},{1,2},{2,3},{3,4},{4,5},{5,6},{6,7},{8,9},{9,10},{10,11},{11... | collective-permute-start | bytes 1572872 | tf_op jit(solution)/shard_map/ppermute | solution.py:17
  149.9 2.0 copy.42
  156.0 2.7 fusion.14
  158.8 4.1 %fusion.59 = (bf16[16,128,640]{2,1,0:T(8,128)(2,1)}, f32[16,128]{1,0:T(8,128)S(1)}, f32[16,128,640]{2,1,0:T(8,128)S(1)}) fusion(f32[16,128]{1,0:T(8,128)S(1)} %get-tuple-element.51, f32[16,128,640]{2,1,0:T(8,128)S(1)} %get-tuple-element.52, pred[128,640]{1,0:T(8,128)(4,1)S(1)} %get-tuple-element.45, f32[16,128]{1,0:T(8,128)S(1)} %multiply_divide_fusion, ...), kind=kOutput, calls=%fused_computation.121 | convolution fusion | flops 345241600 | bytes 16367616 | tf_op jit(solution)/shard_map/transpose(jvp(hqk,khe->qhe))/dot_general | solution.py:53
  162.9 3.4 %multiply_reduce_fusion.1 = (f32[16,128]{1,0:T(8,128)S(1)}, f32[128,16,128]{0,2,1:T(8,128)S(1)}) fusion(f32[640,16,128]{0,2,1:T(8,128)S(1)} %get-tuple-element.29, f32[16,128]{1,0:T(8,128)S(1)} %bitcast.104, bf16[640,16,128]{0,2,1:T(8,128)(2,1)S(1)} %get-tuple-element.30, bf16[640,16,128]{0,2,1:T(8,128)(2,1)S(1)} %constant_dynamic-update-slice_fusion.7, ...), kind=kOutput, calls=%fused_computation.58 | convolution fusion | flops 352057344 | bytes 17989632 | tf_op jit(solution)/shard_map/transpose(jvp(qhe,khe->hqk))/dot_general | solution.py:40
  166.3 3.9 %fusion.6 = (f32[16,128]{1,0:T(8,128)S(1)}, f32[640,16]{0,1:T(8,128)S(1)}, f32[16,640,128]{1,2,0:T(8,128)S(1)}) fusion(bf16[640,16,128]{0,2,1:T(8,128)(2,1)S(1)} %constant_dynamic-update-slice_fusion.7, f32[640,16]{0,1:T(8,128)S(1)} %fusion.54, f32[128,16,128]{0,2,1:T(8,128)S(1)} %get-tuple-element.38, f32[16,128]{1,0:T(8,128)S(1)} %bitcast.100, ...), kind=kOutput, calls=%fused_computation.19 | convolution fusion | flops 354930688 | bytes 21176320 | tf_op jit(solution)/shard_map/transpose(jvp(qhe,khe->hqk))/dot_general | solution.py:40
  170.3 4.0 %fusion.27 = f32[16,128]{1,0:T(8,128)S(1)} fusion(f32[128,16,128]{2,0,1:T(8,128)S(1)} %copy-done.2, bf16[640,16,128]{0,2,1:T(8,128)(2,1)S(1)} %constant_dynamic-update-slice_fusion.7, bf16[16,128,640]{2,1,0:T(8,128)(2,1)} %get-tuple-element.27, f32[16,128,640]{2,1,0:T(8,128)S(1)} %get-tuple-element.52, f32[16,128]{1,0:T(8,128)S(1)} %get-tuple-element.51, ...), kind=kOutput, calls=%fused_computation.50 | convolution fusion | flops 343930880 | bytes 11632640 | tf_op jit(solution)/shard_map/jvp(hqk,khe->qhe)/dot_general | solution.py:53
  174.3 4.9 %add_add_fusion = f32[640,16,128]{0,2,1:T(8,128)} fusion(bf16[640,16,128]{0,2,1:T(8,128)(2,1)S(1)} %constant_dynamic-update-slice_fusion.7, f32[128,16,128]{0,2,1:T(8,128)S(1)} %get-tuple-element.38, f32[16,640,128]{1,2,0:T(8,128)S(1)} %get-tuple-element.54, f32[640,16]{0,1:T(8,128)S(1)} %multiply_multiply_fusion.1, f32[16,128]{1,0:T(8,128)S(1)} %bitcast.101, ...), kind=kOutput, calls=%fused_computation.4 | convolution fusion | flops 354418688 | bytes 22732800 | tf_op jit(solution)/shard_map/transpose(jvp(hqk,khe->qhe))/dot_general | solution.py:53
  179.2 6.0 %copy.48 = f32[640,2048]{1,0:T(8,128)} copy(f32[640,2048]{0,1:T(8,128)} %bitcast.70) | data formatting | bytes 10485760 | tf_op jit(solution)/shard_map/transpose(jvp())/reshape | solution.py:34
  185.1 6.1 %fusion.60 = (bf16[640,2048]{1,0:T(8,128)(2,1)S(1)}, f32[640,2048]{1,0:T(8,128)}) fusion(f32[640,2048]{1,0:T(8,128)} %copy.48, bf16[128,2048]{1,0:T(8,128)(2,1)S(1)} %bitcast.84), kind=kLoop, calls=%fused_computation.122 | loop fusion | flops 3932160 | bytes 13631488 | tf_op jit(solution)/shard_map/convert.8
  195.4 2.0 copy.30
  202.2 2.0 copy.32
  207.8 2.0 copy.33
  212.9 2.8 fusion.12
  216.8 3.3 %fusion.2 = f32[16,128,128]{2,1,0:T(8,128)} fusion(bf16[640,16,128]{0,2,1:T(8,128)(2,1)S(1)} %constant_dynamic-update-slice_fusion, bf16[16,128,640]{2,1,0:T(8,128)(2,1)S(1)} %fusion.29, f32[16,128,640]{2,1,0:T(8,128)S(1)} %get-tuple-element.50, f32[16,128]{1,0:T(8,128)S(1)} %get-tuple-element.49, pred[128,640]{1,0:T(8,128)(4,1)S(1)} %get-tuple-element.46), kind=kOutput, calls=%fused_computation.13 | convolution fusion | flops 343408640 | bytes 11624448 | tf_op jit(solution)/shard_map/hqk,khe->qhe/dot_general | solution.py:53
  223.0 21.3 %collective-permute-done.20 = bf16[128,2048]{1,0:T(8,128)(2,1)} collective-permute-done((bf16[128,2048]{1,0:T(8,128)(2,1)}, bf16[128,2048]{1,0:T(8,128)(2,1)}, u32[]{:S(2)}, u32[]{:S(2)}) %collective-permute-start.20) | collective-permute-done | bytes 524320 | tf_op jit(solution)/shard_map/ppermute | solution.py:17
  244.3 2.2 fusion.30
  246.6 71.7 %psum.7 = f32[3,2048]{1,0:T(4,128)S(1)} all-reduce(f32[3,2048]{1,0:T(4,128)S(1)} %pad_add_fusion), channel_id=1, replica_groups=mesh['dp'=2,'pipe'=2,'ctx'=8] {'dp','ctx'}, use_global_device_ids=true, to_apply=%region_9.10 | all-reduce | flops 6144 | bytes 49152 | tf_op jit(solution)/shard_map/psum | solution.py:119
  (102 shorter events, 56.2 us)
Async XLA Ops:
  0.6 135.2 %collective-permute-start.13 = (bf16[128,2048]{1,0:T(8,128)(2,1)}, bf16[128,2048]{1,0:T(8,128)(2,1)S(1)}, u32[]{:S(2)}, u32[]{:S(2)}) collective-permute-start(bf16[128,2048]{1,0:T(8,128)(2,1)} %bitcast.86), channel_id=1, source_target_pairs={{0,4},{1,5},{2,6},{3,7},{8,12},{9,13},{10,14},{11,15},{16,20},{17,... | collective-permute-start | bytes 1572872 | tf_op jit(solution)/shard_map/ppermute | solution.py:17
  6.6 132.3 %collective-permute-start.14 = (bf16[128,2048]{1,0:T(8,128)(2,1)}, bf16[128,2048]{1,0:T(8,128)(2,1)S(1)}, u32[]{:S(2)}, u32[]{:S(2)}) collective-permute-start(bf16[128,2048]{1,0:T(8,128)(2,1)} %bitcast.87), channel_id=1, source_target_pairs={{0,3},{1,4},{2,5},{3,6},{4,7},{8,11},{9,12},{10,13},{11,14},{12,15... | collective-permute-start | bytes 1572872 | tf_op jit(solution)/shard_map/ppermute | solution.py:17
  11.1 130.9 %collective-permute-start.15 = (bf16[128,2048]{1,0:T(8,128)(2,1)}, bf16[128,2048]{1,0:T(8,128)(2,1)S(1)}, u32[]{:S(2)}, u32[]{:S(2)}) collective-permute-start(bf16[128,2048]{1,0:T(8,128)(2,1)} %bitcast.88), channel_id=1, source_target_pairs={{0,2},{1,3},{2,4},{3,5},{4,6},{5,7},{8,10},{9,11},{10,12},{11,13},... | collective-permute-start | bytes 1572872 | tf_op jit(solution)/shard_map/ppermute | solution.py:17
  12.4 137.4 %collective-permute-start.16 = (bf16[128,2048]{1,0:T(8,128)(2,1)}, bf16[128,2048]{1,0:T(8,128)(2,1)}, u32[]{:S(2)}, u32[]{:S(2)}) collective-permute-start(bf16[128,2048]{1,0:T(8,128)(2,1)} %bitcast.89), channel_id=1, source_target_pairs={{0,1},{1,2},{2,3},{3,4},{4,5},{5,6},{6,7},{8,9},{9,10},{10,11},{11... | collective-permute-start | bytes 1572872 | tf_op jit(solution)/shard_map/ppermute | solution.py:17
  16.3 24.3 %collective-permute-start.4 = (s32[128]{0:T(128)}, s32[128]{0:T(128)S(1)}, u32[]{:S(2)}, u32[]{:S(2)}) collective-permute-start(s32[128]{0:T(128)} %bitcast.116), channel_id=1, source_target_pairs={{0,4},{1,5},{2,6},{3,7},{8,12},{9,13},{10,14},{11,15},{16,20},{17,... | collective-permute-start | bytes 1544 | tf_op jit(solution)/shard_map/ppermute | solution.py:17
  40.6 39.4 %collective-permute-start.5 = (s32[128]{0:T(128)}, s32[128]{0:T(128)S(1)}, u32[]{:S(2)}, u32[]{:S(2)}) collective-permute-start(s32[128]{0:T(128)} %bitcast.117), channel_id=1, source_target_pairs={{0,3},{1,4},{2,5},{3,6},{4,7},{8,11},{9,12},{10,13},{11,14},{12,15... | collective-permute-start | bytes 1544 | tf_op jit(solution)/shard_map/ppermute | solution.py:17
  80.0 2.7 collective-permute-start.6
  82.7 7.6 %collective-permute-start.7 = (s32[128]{0:T(128)}, s32[128]{0:T(128)S(1)}, u32[]{:S(2)}, u32[]{:S(2)}) collective-permute-start(s32[128]{0:T(128)} %bitcast.119), channel_id=1, source_target_pairs={{0,1},{1,2},{2,3},{3,4},{4,5},{5,6},{6,7},{8,9},{9,10},{10,11},{11... | collective-permute-start | bytes 1544 | tf_op jit(solution)/shard_map/ppermute | solution.py:17
  90.4 8.2 %collective-permute-start.9 = (s32[128]{0:T(128)}, s32[128]{0:T(128)S(1)}, u32[]{:S(2)}, u32[]{:S(2)}) collective-permute-start(s32[128]{0:T(128)} %bitcast.111), channel_id=1, source_target_pairs={{0,4},{1,5},{2,6},{3,7},{8,12},{9,13},{10,14},{11,15},{16,20},{17,... | collective-permute-start | bytes 1544 | tf_op jit(solution)/shard_map/ppermute | solution.py:17
  98.6 5.6 %collective-permute-start.10 = (s32[128]{0:T(128)}, s32[128]{0:T(128)S(1)}, u32[]{:S(2)}, u32[]{:S(2)}) collective-permute-start(s32[128]{0:T(128)} %bitcast.112), channel_id=1, source_target_pairs={{0,3},{1,4},{2,5},{3,6},{4,7},{8,11},{9,12},{10,13},{11,14},{12,15... | collective-permute-start | bytes 1544 | tf_op jit(solution)/shard_map/ppermute | solution.py:17
  104.2 4.8 %collective-permute-start.11 = (s32[128]{0:T(128)}, s32[128]{0:T(128)S(1)}, u32[]{:S(2)}, u32[]{:S(2)}) collective-permute-start(s32[128]{0:T(128)} %bitcast.113), channel_id=1, source_target_pairs={{0,2},{1,3},{2,4},{3,5},{4,6},{5,7},{8,10},{9,11},{10,12},{11,13},... | collective-permute-start | bytes 1544 | tf_op jit(solution)/shard_map/ppermute | solution.py:17
  109.0 5.6 %collective-permute-start.12 = (s32[128]{0:T(128)}, s32[128]{0:T(128)S(1)}, u32[]{:S(2)}, u32[]{:S(2)}) collective-permute-start(s32[128]{0:T(128)} %bitcast.114), channel_id=1, source_target_pairs={{0,1},{1,2},{2,3},{3,4},{4,5},{5,6},{6,7},{8,9},{9,10},{10,11},{11... | collective-permute-start | bytes 1544 | tf_op jit(solution)/shard_map/ppermute | solution.py:17
  114.5 79.5 %collective-permute-start = (bf16[128,2048]{1,0:T(8,128)(2,1)}, bf16[128,2048]{1,0:T(8,128)(2,1)}, u32[]{:S(2)}, u32[]{:S(2)}) collective-permute-start(bf16[128,2048]{1,0:T(8,128)(2,1)} %bitcast), channel_id=1, source_target_pairs={{0,4},{1,5},{2,6},{3,7},{8,12},{9,13},{10,14},{11,15},{16,20},{17,... | collective-permute-start | bytes 1572872 | tf_op jit(solution)/shard_map/ppermute | solution.py:17
  135.8 61.6 %collective-permute-start.1 = (bf16[128,2048]{1,0:T(8,128)(2,1)}, bf16[128,2048]{1,0:T(8,128)(2,1)}, u32[]{:S(2)}, u32[]{:S(2)}) collective-permute-start(bf16[128,2048]{1,0:T(8,128)(2,1)} %bitcast), channel_id=1, source_target_pairs={{0,3},{1,4},{2,5},{3,6},{4,7},{8,11},{9,12},{10,13},{11,14},{12,15... | collective-permute-start | bytes 1572872 | tf_op jit(solution)/shard_map/ppermute | solution.py:17
  138.9 62.1 %collective-permute-start.2 = (bf16[128,2048]{1,0:T(8,128)(2,1)}, bf16[128,2048]{1,0:T(8,128)(2,1)}, u32[]{:S(2)}, u32[]{:S(2)}) collective-permute-start(bf16[128,2048]{1,0:T(8,128)(2,1)} %bitcast), channel_id=1, source_target_pairs={{0,2},{1,3},{2,4},{3,5},{4,6},{5,7},{8,10},{9,11},{10,12},{11,13},... | collective-permute-start | bytes 1572872 | tf_op jit(solution)/shard_map/ppermute | solution.py:17
  142.0 65.8 %collective-permute-start.3 = (bf16[128,2048]{1,0:T(8,128)(2,1)}, bf16[128,2048]{1,0:T(8,128)(2,1)}, u32[]{:S(2)}, u32[]{:S(2)}) collective-permute-start(bf16[128,2048]{1,0:T(8,128)(2,1)} %bitcast), channel_id=1, source_target_pairs={{0,1},{1,2},{2,3},{3,4},{4,5},{5,6},{6,7},{8,9},{9,10},{10,11},{11... | collective-permute-start | bytes 1572872 | tf_op jit(solution)/shard_map/ppermute | solution.py:17
  166.3 3.9 %copy-start.2 = (f32[128,16,128]{2,0,1:T(8,128)S(1)}, f32[128,16,128]{2,0,1:T(8,128)}, u32[]{:S(2)}) copy-start(f32[128,16,128]{2,0,1:T(8,128)} %copy.50) | copy-start | bytes 3145732
  170.3 4.0 %copy-start.3 = (bf16[16,128,640]{2,1,0:T(8,128)(2,1)S(1)}, bf16[16,128,640]{2,1,0:T(8,128)(2,1)}, u32[]{:S(2)}) copy-start(bf16[16,128,640]{2,1,0:T(8,128)(2,1)} %get-tuple-element.27) | copy-start | bytes 7864324
  179.2 6.0 %copy-start.1 = (bf16[1,1,128,2048]{3,2,1,0:T(8,128)(2,1)S(1)}, bf16[1,1,128,2048]{3,2,1,0:T(8,128)(2,1)}, u32[]{:S(2)}) copy-start(bf16[1,1,128,2048]{3,2,1,0:T(8,128)(2,1)} %param.16) | copy-start | bytes 1572868
  192.6 18.4 %copy-start = (bf16[1,1,128,2048]{2,3,1,0:T(8,128)(2,1)S(1)}, bf16[1,1,128,2048]{2,3,1,0:T(8,128)(2,1)}, u32[]{:S(2)}) copy-start(bf16[1,1,128,2048]{2,3,1,0:T(8,128)(2,1)} %copy.34) | copy-start | bytes 1572868
  192.6 30.3 %collective-permute-start.17 = (bf16[128,2048]{1,0:T(8,128)(2,1)}, bf16[128,2048]{1,0:T(8,128)(2,1)}, u32[]{:S(2)}, u32[]{:S(2)}) collective-permute-start(bf16[128,2048]{1,0:T(8,128)(2,1)} %get-tuple-element.33), channel_id=1, source_target_pairs={{1,0},{2,1},{3,2},{4,3},{5,4},{6,5},{7,6},{9,8},{10,9},{11,10},{12... | collective-permute-start | bytes 1572872 | tf_op jit(solution)/shard_map/ppermute | solution.py:17
  194.1 28.9 %collective-permute-start.18 = (bf16[128,2048]{1,0:T(8,128)(2,1)}, bf16[128,2048]{1,0:T(8,128)(2,1)}, u32[]{:S(2)}, u32[]{:S(2)}) collective-permute-start(bf16[128,2048]{1,0:T(8,128)(2,1)} %get-tuple-element.36), channel_id=1, source_target_pairs={{2,0},{3,1},{4,2},{5,3},{6,4},{7,5},{10,8},{11,9},{12,10},{13,11},... | collective-permute-start | bytes 1572872 | tf_op jit(solution)/shard_map/ppermute | solution.py:17
  197.4 25.6 %collective-permute-start.19 = (bf16[128,2048]{1,0:T(8,128)(2,1)}, bf16[128,2048]{1,0:T(8,128)(2,1)}, u32[]{:S(2)}, u32[]{:S(2)}) collective-permute-start(bf16[128,2048]{1,0:T(8,128)(2,1)} %get-tuple-element.35), channel_id=1, source_target_pairs={{3,0},{4,1},{5,2},{6,3},{7,4},{11,8},{12,9},{13,10},{14,11},{15,12... | collective-permute-start | bytes 1572872 | tf_op jit(solution)/shard_map/ppermute | solution.py:17
  201.0 43.3 %collective-permute-start.20 = (bf16[128,2048]{1,0:T(8,128)(2,1)}, bf16[128,2048]{1,0:T(8,128)(2,1)}, u32[]{:S(2)}, u32[]{:S(2)}) collective-permute-start(bf16[128,2048]{1,0:T(8,128)(2,1)} %get-tuple-element.34), channel_id=1, source_target_pairs={{4,0},{5,1},{6,2},{7,3},{12,8},{13,9},{14,10},{15,11},{20,16},{21,... | collective-permute-start | bytes 1572872 | tf_op jit(solution)/shard_map/ppermute | solution.py:17
  222.9 96.1 %collective-permute-start.8 = (bf16[128,2048]{1,0:T(8,128)(2,1)S(1)}, bf16[128,2048]{1,0:T(8,128)(2,1)S(1)}, u32[]{:S(2)}, u32[]{:S(2)}) collective-permute-start(bf16[128,2048]{1,0:T(8,128)(2,1)S(1)} %add_convert_fusion), channel_id=1, source_target_pairs={{0,8},{8,0},{1,9},{9,1},{2,10},{10,2},{3,11},{11,3},{4,12},{12,4},... | collective-permute-start | bytes 1572872 | tf_op jit(solution)/shard_map/ppermute | solution.py:23
  246.5 72.5 %collective-permute-start.21 = (bf16[128,2048]{1,0:T(8,128)(2,1)S(1)}, bf16[128,2048]{1,0:T(8,128)(2,1)S(1)}, u32[]{:S(2)}, u32[]{:S(2)}) collective-permute-start(bf16[128,2048]{1,0:T(8,128)(2,1)S(1)} %fusion.30), channel_id=1, source_target_pairs={{0,8},{8,0},{1,9},{9,1},{2,10},{10,2},{3,11},{11,3},{4,12},{12,4},... | collective-permute-start | bytes 1572872 | tf_op jit(solution)/shard_map/ppermute | solution.py:23
where the time goes:
time: 322 us; the launch traced here: 321 us
  starting transfers between devices  114 us (35%)
  blocking collectives  71.7 us (22%)
  local copies, waits for them, and re-layouts  47 us (15%)
  waiting for transfers between devices  39 us (12%)
  matrix products  29.1 us (9%)
  other arithmetic  15.1 us (5%)
  between operations  5.06 us (2%)
    ppermute x20, starting transfers between devices, passed_along(): lax.ppermute(value, axis, [(source, source + steps) for source in range(f...  113 us
    psum x1, blocking collectives, local(): gain_total = lax.psum(gain_grads, ('dp', 'ctx'))  71.7 us
    ppermute x20, waiting for transfers between devices, passed_along(): lax.ppermute(value, axis, [(source, source + steps) for source in range(f...  39 us
    unnamed x33, local copies, waits for them, and re-layouts  17.3 us
    dot_general x4, matrix products, attend(): mixture = jnp.einsum('hqk,khe->qhe', probability, shaped)  16.3 us
    ppermute x8, local copies, waits for them, and re-layouts, passed_along(): lax.ppermute(value, axis, [(source, source + steps) for source in range(f...  13.2 us
    dot_general x4, matrix products, attend(): jnp.einsum('qhe,khe->hqk', queries, key_vecs)  12.8 us
  transfers between devices with their start and end apart: 22, of which 9 were waited for; matrix products, arithmetic and copies ran while one was open for 28% of the time, Pallas kernels for 0%

commit v1 on v0

--- a/solution.py
+++ b/solution.py
@@ -116,7 +116,7 @@
         arriving = arriving + passed_along(outgoing, "ctx", -reach).astype(jnp.float32)
     own_grads = own_grads.at[shard_rows - piece_len :].add(arriving)
     upstream_grad = shifted(own_grads.astype(jnp.bfloat16), "pipe", -1)
-    gain_total = lax.psum(gain_grads, ("dp", "ctx"))
+    gain_total = lax.psum(lax.psum(gain_grads, "ctx"), "dp")
     gain_total = gain_total / jnp.float32(TOK_DEV)
     return (next_input[None, None], upstream_grad[None, None], gain_total[None])
 

time: 322 us -> 292 us (0.907)
  blocking collectives: 71.7 us -> 41.4 us
    psum x1 -> x2, blocking collectives: 71.7 us -> 41.4 us  [local(): gain_total = lax.psum(lax.psum(gain_grads, 'ctx'), 'dp')]
  transfers between devices with their start and end apart: 22 -> 22, of which waited for: 9 -> 9; matrix products, arithmetic and copies ran while one was open for 28% -> 31% of each run, Pallas kernels for 0% -> 0%
where the time goes in v1:
time: 292 us; the launch traced here: 290 us
  starting transfers between devices  114 us (39%)
  local copies, waits for them, and re-layouts  47.1 us (16%)
  blocking collectives  41.4 us (14%)
  waiting for transfers between devices  38.9 us (13%)
  matrix products  29.1 us (10%)
  other arithmetic  15.1 us (5%)
  between operations  5.07 us (2%)
    ppermute x20, starting transfers between devices, passed_along(): lax.ppermute(value, axis, [(source, source + steps) for source in range(f...  113 us
    psum x2, blocking collectives, local(): gain_total = lax.psum(lax.psum(gain_grads, 'ctx'), 'dp')  41.4 us
    ppermute x20, waiting for transfers between devices, passed_along(): lax.ppermute(value, axis, [(source, source + steps) for source in range(f...  38.9 us
    unnamed x33, local copies, waits for them, and re-layouts  17.3 us
    dot_general x4, matrix products, attend(): mixture = jnp.einsum('hqk,khe->qhe', probability, shaped)  16.4 us
    ppermute x8, local copies, waits for them, and re-layouts, passed_along(): lax.ppermute(value, axis, [(source, source + steps) for source in range(f...  13.2 us
    dot_general x4, matrix products, attend(): jnp.einsum('qhe,khe->hqk', queries, key_vecs)  12.8 us
    another operation x1, other arithmetic  6.1 us
  transfers between devices with their start and end apart: 22, of which 9 were waited for; matrix products, arithmetic and copies ran while one was open for 31% of the time, Pallas kernels for 0%

profile of v1, /device:TPU:0, one launch (start us, length us, event | category | flops | bytes accessed | tf_op | source)
XLA Modules:
  0.0 290.2 jit_solution(6523721736747936232)
XLA Ops:
  0.6 6.0 %collective-permute-start.13 = (bf16[128,2048]{1,0:T(8,128)(2,1)}, bf16[128,2048]{1,0:T(8,128)(2,1)S(1)}, u32[]{:S(2)}, u32[]{:S(2)}) collective-permute-start(bf16[128,2048]{1,0:T(8,128)(2,1)} %bitcast.86), channel_id=1, source_target_pairs={{0,4},{1,5},{2,6},{3,7},{8,12},{9,13},{10,14},{11,15},{16,20},{17,... | collective-permute-start | bytes 1572872 | tf_op jit(solution)/shard_map/ppermute | solution.py:17
  6.6 4.5 %collective-permute-start.14 = (bf16[128,2048]{1,0:T(8,128)(2,1)}, bf16[128,2048]{1,0:T(8,128)(2,1)S(1)}, u32[]{:S(2)}, u32[]{:S(2)}) collective-permute-start(bf16[128,2048]{1,0:T(8,128)(2,1)} %bitcast.87), channel_id=1, source_target_pairs={{0,3},{1,4},{2,5},{3,6},{4,7},{8,11},{9,12},{10,13},{11,14},{12,15... | collective-permute-start | bytes 1572872 | tf_op jit(solution)/shard_map/ppermute | solution.py:17
  12.4 3.9 %collective-permute-start.16 = (bf16[128,2048]{1,0:T(8,128)(2,1)}, bf16[128,2048]{1,0:T(8,128)(2,1)}, u32[]{:S(2)}, u32[]{:S(2)}) collective-permute-start(bf16[128,2048]{1,0:T(8,128)(2,1)} %bitcast.89), channel_id=1, source_target_pairs={{0,1},{1,2},{2,3},{3,4},{4,5},{5,6},{6,7},{8,9},{9,10},{10,11},{11... | collective-permute-start | bytes 1572872 | tf_op jit(solution)/shard_map/ppermute | solution.py:17
  21.5 2.0 copy.43
  26.1 2.1 copy.34
  32.1 8.5 %collective-permute-done.4 = s32[128]{0:T(128)S(1)} collective-permute-done((s32[128]{0:T(128)}, s32[128]{0:T(128)S(1)}, u32[]{:S(2)}, u32[]{:S(2)}) %collective-permute-start.4) | collective-permute-done | bytes 544 | tf_op jit(solution)/shard_map/ppermute | solution.py:17
  40.6 38.0 %collective-permute-start.5 = (s32[128]{0:T(128)}, s32[128]{0:T(128)S(1)}, u32[]{:S(2)}, u32[]{:S(2)}) collective-permute-start(s32[128]{0:T(128)} %bitcast.117), channel_id=1, source_target_pairs={{0,3},{1,4},{2,5},{3,6},{4,7},{8,11},{9,12},{10,13},{11,14},{12,15... | collective-permute-start | bytes 1544 | tf_op jit(solution)/shard_map/ppermute | solution.py:17
  82.7 6.2 %collective-permute-start.7 = (s32[128]{0:T(128)}, s32[128]{0:T(128)S(1)}, u32[]{:S(2)}, u32[]{:S(2)}) collective-permute-start(s32[128]{0:T(128)} %bitcast.119), channel_id=1, source_target_pairs={{0,1},{1,2},{2,3},{3,4},{4,5},{5,6},{6,7},{8,9},{9,10},{10,11},{11... | collective-permute-start | bytes 1544 | tf_op jit(solution)/shard_map/ppermute | solution.py:17
  90.4 6.8 %collective-permute-start.9 = (s32[128]{0:T(128)}, s32[128]{0:T(128)S(1)}, u32[]{:S(2)}, u32[]{:S(2)}) collective-permute-start(s32[128]{0:T(128)} %bitcast.111), channel_id=1, source_target_pairs={{0,4},{1,5},{2,6},{3,7},{8,12},{9,13},{10,14},{11,15},{16,20},{17,... | collective-permute-start | bytes 1544 | tf_op jit(solution)/shard_map/ppermute | solution.py:17
  98.6 4.1 %collective-permute-start.10 = (s32[128]{0:T(128)}, s32[128]{0:T(128)S(1)}, u32[]{:S(2)}, u32[]{:S(2)}) collective-permute-start(s32[128]{0:T(128)} %bitcast.112), channel_id=1, source_target_pairs={{0,3},{1,4},{2,5},{3,6},{4,7},{8,11},{9,12},{10,13},{11,14},{12,15... | collective-permute-start | bytes 1544 | tf_op jit(solution)/shard_map/ppermute | solution.py:17
  104.2 3.4 %collective-permute-start.11 = (s32[128]{0:T(128)}, s32[128]{0:T(128)S(1)}, u32[]{:S(2)}, u32[]{:S(2)}) collective-permute-start(s32[128]{0:T(128)} %bitcast.113), channel_id=1, source_target_pairs={{0,2},{1,3},{2,4},{3,5},{4,6},{5,7},{8,10},{9,11},{10,12},{11,13},... | collective-permute-start | bytes 1544 | tf_op jit(solution)/shard_map/ppermute | solution.py:17
  109.0 4.1 %collective-permute-start.12 = (s32[128]{0:T(128)}, s32[128]{0:T(128)S(1)}, u32[]{:S(2)}, u32[]{:S(2)}) collective-permute-start(s32[128]{0:T(128)} %bitcast.114), channel_id=1, source_target_pairs={{0,1},{1,2},{2,3},{3,4},{4,5},{5,6},{6,7},{8,9},{9,10},{10,11},{11... | collective-permute-start | bytes 1544 | tf_op jit(solution)/shard_map/ppermute | solution.py:17
  114.5 19.6 %collective-permute-start = (bf16[128,2048]{1,0:T(8,128)(2,1)}, bf16[128,2048]{1,0:T(8,128)(2,1)}, u32[]{:S(2)}, u32[]{:S(2)}) collective-permute-start(bf16[128,2048]{1,0:T(8,128)(2,1)} %bitcast), channel_id=1, source_target_pairs={{0,4},{1,5},{2,6},{3,7},{8,12},{9,13},{10,14},{11,15},{16,20},{17,... | collective-permute-start | bytes 1572872 | tf_op jit(solution)/shard_map/ppermute | solution.py:17
  135.8 2.1 collective-permute-start.1
  138.9 2.1 collective-permute-start.2
  142.0 3.4 %collective-permute-start.3 = (bf16[128,2048]{1,0:T(8,128)(2,1)}, bf16[128,2048]{1,0:T(8,128)(2,1)}, u32[]{:S(2)}, u32[]{:S(2)}) collective-permute-start(bf16[128,2048]{1,0:T(8,128)(2,1)} %bitcast), channel_id=1, source_target_pairs={{0,1},{1,2},{2,3},{3,4},{4,5},{5,6},{6,7},{8,9},{9,10},{10,11},{11... | collective-permute-start | bytes 1572872 | tf_op jit(solution)/shard_map/ppermute | solution.py:17
  156.0 2.7 fusion.14
  158.8 4.1 %fusion.59 = (bf16[16,128,640]{2,1,0:T(8,128)(2,1)}, f32[16,128]{1,0:T(8,128)S(1)}, f32[16,128,640]{2,1,0:T(8,128)S(1)}) fusion(f32[16,128]{1,0:T(8,128)S(1)} %get-tuple-element.51, f32[16,128,640]{2,1,0:T(8,128)S(1)} %get-tuple-element.52, pred[128,640]{1,0:T(8,128)(4,1)S(1)} %get-tuple-element.45, f32[16,128]{1,0:T(8,128)S(1)} %multiply_divide_fusion, ...), kind=kOutput, calls=%fused_computation.121 | convolution fusion | flops 345241600 | bytes 16367616 | tf_op jit(solution)/shard_map/transpose(jvp(hqk,khe->qhe))/dot_general | solution.py:53
  162.9 3.4 %multiply_reduce_fusion.1 = (f32[16,128]{1,0:T(8,128)S(1)}, f32[128,16,128]{0,2,1:T(8,128)S(1)}) fusion(f32[640,16,128]{0,2,1:T(8,128)S(1)} %get-tuple-element.29, f32[16,128]{1,0:T(8,128)S(1)} %bitcast.104, bf16[640,16,128]{0,2,1:T(8,128)(2,1)S(1)} %get-tuple-element.30, bf16[640,16,128]{0,2,1:T(8,128)(2,1)S(1)} %constant_dynamic-update-slice_fusion.7, ...), kind=kOutput, calls=%fused_computation.58 | convolution fusion | flops 352057344 | bytes 17989632 | tf_op jit(solution)/shard_map/transpose(jvp(qhe,khe->hqk))/dot_general | solution.py:40
  166.3 3.9 %fusion.6 = (f32[16,128]{1,0:T(8,128)S(1)}, f32[640,16]{0,1:T(8,128)S(1)}, f32[16,640,128]{1,2,0:T(8,128)S(1)}) fusion(bf16[640,16,128]{0,2,1:T(8,128)(2,1)S(1)} %constant_dynamic-update-slice_fusion.7, f32[640,16]{0,1:T(8,128)S(1)} %fusion.54, f32[128,16,128]{0,2,1:T(8,128)S(1)} %get-tuple-element.38, f32[16,128]{1,0:T(8,128)S(1)} %bitcast.100, ...), kind=kOutput, calls=%fused_computation.19 | convolution fusion | flops 354930688 | bytes 21176320 | tf_op jit(solution)/shard_map/transpose(jvp(qhe,khe->hqk))/dot_general | solution.py:40
  170.3 4.0 %fusion.27 = f32[16,128]{1,0:T(8,128)S(1)} fusion(f32[128,16,128]{2,0,1:T(8,128)S(1)} %copy-done.2, bf16[640,16,128]{0,2,1:T(8,128)(2,1)S(1)} %constant_dynamic-update-slice_fusion.7, bf16[16,128,640]{2,1,0:T(8,128)(2,1)} %get-tuple-element.27, f32[16,128,640]{2,1,0:T(8,128)S(1)} %get-tuple-element.52, f32[16,128]{1,0:T(8,128)S(1)} %get-tuple-element.51, ...), kind=kOutput, calls=%fused_computation.50 | convolution fusion | flops 343930880 | bytes 11632640 | tf_op jit(solution)/shard_map/jvp(hqk,khe->qhe)/dot_general | solution.py:53
  174.3 4.9 %add_add_fusion = f32[640,16,128]{0,2,1:T(8,128)} fusion(bf16[640,16,128]{0,2,1:T(8,128)(2,1)S(1)} %constant_dynamic-update-slice_fusion.7, f32[128,16,128]{0,2,1:T(8,128)S(1)} %get-tuple-element.38, f32[16,640,128]{1,2,0:T(8,128)S(1)} %get-tuple-element.54, f32[640,16]{0,1:T(8,128)S(1)} %multiply_multiply_fusion.1, f32[16,128]{1,0:T(8,128)S(1)} %bitcast.101, ...), kind=kOutput, calls=%fused_computation.4 | convolution fusion | flops 354418688 | bytes 22732800 | tf_op jit(solution)/shard_map/transpose(jvp(hqk,khe->qhe))/dot_general | solution.py:53
  179.2 6.1 %copy.48 = f32[640,2048]{1,0:T(8,128)} copy(f32[640,2048]{0,1:T(8,128)} %bitcast.70) | data formatting | bytes 10485760 | tf_op jit(solution)/shard_map/transpose(jvp())/reshape | solution.py:34
  185.2 6.1 %fusion.60 = (bf16[640,2048]{1,0:T(8,128)(2,1)S(1)}, f32[640,2048]{1,0:T(8,128)}) fusion(f32[640,2048]{1,0:T(8,128)} %copy.48, bf16[128,2048]{1,0:T(8,128)(2,1)S(1)} %bitcast.84), kind=kLoop, calls=%fused_computation.122 | loop fusion | flops 3932160 | bytes 13631488 | tf_op jit(solution)/shard_map/convert.8
  195.5 2.0 copy.30
  202.3 2.0 copy.32
  213.0 2.8 fusion.12
  216.9 3.4 %fusion.2 = f32[16,128,128]{2,1,0:T(8,128)} fusion(bf16[640,16,128]{0,2,1:T(8,128)(2,1)S(1)} %constant_dynamic-update-slice_fusion, bf16[16,128,640]{2,1,0:T(8,128)(2,1)S(1)} %fusion.29, f32[16,128,640]{2,1,0:T(8,128)S(1)} %get-tuple-element.50, f32[16,128]{1,0:T(8,128)S(1)} %get-tuple-element.49, pred[128,640]{1,0:T(8,128)(4,1)S(1)} %get-tuple-element.46), kind=kOutput, calls=%fused_computation.13 | convolution fusion | flops 343408640 | bytes 11624448 | tf_op jit(solution)/shard_map/hqk,khe->qhe/dot_general | solution.py:53
  223.1 21.2 %collective-permute-done.20 = bf16[128,2048]{1,0:T(8,128)(2,1)} collective-permute-done((bf16[128,2048]{1,0:T(8,128)(2,1)}, bf16[128,2048]{1,0:T(8,128)(2,1)}, u32[]{:S(2)}, u32[]{:S(2)}) %collective-permute-start.20) | collective-permute-done | bytes 524320 | tf_op jit(solution)/shard_map/ppermute | solution.py:17
  244.3 2.2 fusion.30
  246.7 33.0 %psum.14 = f32[3,2048]{1,0:T(4,128)S(1)} all-reduce(f32[3,2048]{1,0:T(4,128)S(1)} %pad_add_fusion), channel_id=1, replica_groups=mesh['dp'=2,'pipe'=2,'ctx'=8] {'ctx'}, use_global_device_ids=true, to_apply=%region_9.10 | all-reduce | flops 6144 | bytes 49152 | tf_op jit(solution)/shard_map/psum | solution.py:119
  279.7 8.3 %psum.15 = f32[3,2048]{1,0:T(4,128)S(1)} all-reduce(f32[3,2048]{1,0:T(4,128)S(1)} %psum.14), channel_id=1, replica_groups=mesh['dp'=2,'pipe'=2,'ctx'=8] {'dp'}, use_global_device_ids=true, to_apply=%region_10.11 | all-reduce | flops 6144 | bytes 49152 | tf_op jit(solution)/shard_map/psum | solution.py:119
  (103 shorter events, 58.2 us)
Async XLA Ops:
  0.6 135.2 %collective-permute-start.13 = (bf16[128,2048]{1,0:T(8,128)(2,1)}, bf16[128,2048]{1,0:T(8,128)(2,1)S(1)}, u32[]{:S(2)}, u32[]{:S(2)}) collective-permute-start(bf16[128,2048]{1,0:T(8,128)(2,1)} %bitcast.86), channel_id=1, source_target_pairs={{0,4},{1,5},{2,6},{3,7},{8,12},{9,13},{10,14},{11,15},{16,20},{17,... | collective-permute-start | bytes 1572872 | tf_op jit(solution)/shard_map/ppermute | solution.py:17
  6.6 132.3 %collective-permute-start.14 = (bf16[128,2048]{1,0:T(8,128)(2,1)}, bf16[128,2048]{1,0:T(8,128)(2,1)S(1)}, u32[]{:S(2)}, u32[]{:S(2)}) collective-permute-start(bf16[128,2048]{1,0:T(8,128)(2,1)} %bitcast.87), channel_id=1, source_target_pairs={{0,3},{1,4},{2,5},{3,6},{4,7},{8,11},{9,12},{10,13},{11,14},{12,15... | collective-permute-start | bytes 1572872 | tf_op jit(solution)/shard_map/ppermute | solution.py:17
  11.1 130.9 %collective-permute-start.15 = (bf16[128,2048]{1,0:T(8,128)(2,1)}, bf16[128,2048]{1,0:T(8,128)(2,1)S(1)}, u32[]{:S(2)}, u32[]{:S(2)}) collective-permute-start(bf16[128,2048]{1,0:T(8,128)(2,1)} %bitcast.88), channel_id=1, source_target_pairs={{0,2},{1,3},{2,4},{3,5},{4,6},{5,7},{8,10},{9,11},{10,12},{11,13},... | collective-permute-start | bytes 1572872 | tf_op jit(solution)/shard_map/ppermute | solution.py:17
  12.4 137.4 %collective-permute-start.16 = (bf16[128,2048]{1,0:T(8,128)(2,1)}, bf16[128,2048]{1,0:T(8,128)(2,1)}, u32[]{:S(2)}, u32[]{:S(2)}) collective-permute-start(bf16[128,2048]{1,0:T(8,128)(2,1)} %bitcast.89), channel_id=1, source_target_pairs={{0,1},{1,2},{2,3},{3,4},{4,5},{5,6},{6,7},{8,9},{9,10},{10,11},{11... | collective-permute-start | bytes 1572872 | tf_op jit(solution)/shard_map/ppermute | solution.py:17
  16.3 24.3 %collective-permute-start.4 = (s32[128]{0:T(128)}, s32[128]{0:T(128)S(1)}, u32[]{:S(2)}, u32[]{:S(2)}) collective-permute-start(s32[128]{0:T(128)} %bitcast.116), channel_id=1, source_target_pairs={{0,4},{1,5},{2,6},{3,7},{8,12},{9,13},{10,14},{11,15},{16,20},{17,... | collective-permute-start | bytes 1544 | tf_op jit(solution)/shard_map/ppermute | solution.py:17
  40.6 39.4 %collective-permute-start.5 = (s32[128]{0:T(128)}, s32[128]{0:T(128)S(1)}, u32[]{:S(2)}, u32[]{:S(2)}) collective-permute-start(s32[128]{0:T(128)} %bitcast.117), channel_id=1, source_target_pairs={{0,3},{1,4},{2,5},{3,6},{4,7},{8,11},{9,12},{10,13},{11,14},{12,15... | collective-permute-start | bytes 1544 | tf_op jit(solution)/shard_map/ppermute | solution.py:17
  80.0 2.7 collective-permute-start.6
  82.7 7.6 %collective-permute-start.7 = (s32[128]{0:T(128)}, s32[128]{0:T(128)S(1)}, u32[]{:S(2)}, u32[]{:S(2)}) collective-permute-start(s32[128]{0:T(128)} %bitcast.119), channel_id=1, source_target_pairs={{0,1},{1,2},{2,3},{3,4},{4,5},{5,6},{6,7},{8,9},{9,10},{10,11},{11... | collective-permute-start | bytes 1544 | tf_op jit(solution)/shard_map/ppermute | solution.py:17
  90.4 8.2 %collective-permute-start.9 = (s32[128]{0:T(128)}, s32[128]{0:T(128)S(1)}, u32[]{:S(2)}, u32[]{:S(2)}) collective-permute-start(s32[128]{0:T(128)} %bitcast.111), channel_id=1, source_target_pairs={{0,4},{1,5},{2,6},{3,7},{8,12},{9,13},{10,14},{11,15},{16,20},{17,... | collective-permute-start | bytes 1544 | tf_op jit(solution)/shard_map/ppermute | solution.py:17
  98.6 5.6 %collective-permute-start.10 = (s32[128]{0:T(128)}, s32[128]{0:T(128)S(1)}, u32[]{:S(2)}, u32[]{:S(2)}) collective-permute-start(s32[128]{0:T(128)} %bitcast.112), channel_id=1, source_target_pairs={{0,3},{1,4},{2,5},{3,6},{4,7},{8,11},{9,12},{10,13},{11,14},{12,15... | collective-permute-start | bytes 1544 | tf_op jit(solution)/shard_map/ppermute | solution.py:17
  104.2 4.8 %collective-permute-start.11 = (s32[128]{0:T(128)}, s32[128]{0:T(128)S(1)}, u32[]{:S(2)}, u32[]{:S(2)}) collective-permute-start(s32[128]{0:T(128)} %bitcast.113), channel_id=1, source_target_pairs={{0,2},{1,3},{2,4},{3,5},{4,6},{5,7},{8,10},{9,11},{10,12},{11,13},... | collective-permute-start | bytes 1544 | tf_op jit(solution)/shard_map/ppermute | solution.py:17
  109.0 5.6 %collective-permute-start.12 = (s32[128]{0:T(128)}, s32[128]{0:T(128)S(1)}, u32[]{:S(2)}, u32[]{:S(2)}) collective-permute-start(s32[128]{0:T(128)} %bitcast.114), channel_id=1, source_target_pairs={{0,1},{1,2},{2,3},{3,4},{4,5},{5,6},{6,7},{8,9},{9,10},{10,11},{11... | collective-permute-start | bytes 1544 | tf_op jit(solution)/shard_map/ppermute | solution.py:17
  114.5 79.6 %collective-permute-start = (bf16[128,2048]{1,0:T(8,128)(2,1)}, bf16[128,2048]{1,0:T(8,128)(2,1)}, u32[]{:S(2)}, u32[]{:S(2)}) collective-permute-start(bf16[128,2048]{1,0:T(8,128)(2,1)} %bitcast), channel_id=1, source_target_pairs={{0,4},{1,5},{2,6},{3,7},{8,12},{9,13},{10,14},{11,15},{16,20},{17,... | collective-permute-start | bytes 1572872 | tf_op jit(solution)/shard_map/ppermute | solution.py:17
  135.8 61.7 %collective-permute-start.1 = (bf16[128,2048]{1,0:T(8,128)(2,1)}, bf16[128,2048]{1,0:T(8,128)(2,1)}, u32[]{:S(2)}, u32[]{:S(2)}) collective-permute-start(bf16[128,2048]{1,0:T(8,128)(2,1)} %bitcast), channel_id=1, source_target_pairs={{0,3},{1,4},{2,5},{3,6},{4,7},{8,11},{9,12},{10,13},{11,14},{12,15... | collective-permute-start | bytes 1572872 | tf_op jit(solution)/shard_map/ppermute | solution.py:17
  138.9 62.1 %collective-permute-start.2 = (bf16[128,2048]{1,0:T(8,128)(2,1)}, bf16[128,2048]{1,0:T(8,128)(2,1)}, u32[]{:S(2)}, u32[]{:S(2)}) collective-permute-start(bf16[128,2048]{1,0:T(8,128)(2,1)} %bitcast), channel_id=1, source_target_pairs={{0,2},{1,3},{2,4},{3,5},{4,6},{5,7},{8,10},{9,11},{10,12},{11,13},... | collective-permute-start | bytes 1572872 | tf_op jit(solution)/shard_map/ppermute | solution.py:17
  142.0 65.9 %collective-permute-start.3 = (bf16[128,2048]{1,0:T(8,128)(2,1)}, bf16[128,2048]{1,0:T(8,128)(2,1)}, u32[]{:S(2)}, u32[]{:S(2)}) collective-permute-start(bf16[128,2048]{1,0:T(8,128)(2,1)} %bitcast), channel_id=1, source_target_pairs={{0,1},{1,2},{2,3},{3,4},{4,5},{5,6},{6,7},{8,9},{9,10},{10,11},{11... | collective-permute-start | bytes 1572872 | tf_op jit(solution)/shard_map/ppermute | solution.py:17
  166.3 3.9 %copy-start.2 = (f32[128,16,128]{2,0,1:T(8,128)S(1)}, f32[128,16,128]{2,0,1:T(8,128)}, u32[]{:S(2)}) copy-start(f32[128,16,128]{2,0,1:T(8,128)} %copy.50) | copy-start | bytes 3145732
  170.2 4.0 %copy-start.3 = (bf16[16,128,640]{2,1,0:T(8,128)(2,1)S(1)}, bf16[16,128,640]{2,1,0:T(8,128)(2,1)}, u32[]{:S(2)}) copy-start(bf16[16,128,640]{2,1,0:T(8,128)(2,1)} %get-tuple-element.27) | copy-start | bytes 7864324
  179.2 6.1 %copy-start.1 = (bf16[1,1,128,2048]{3,2,1,0:T(8,128)(2,1)S(1)}, bf16[1,1,128,2048]{3,2,1,0:T(8,128)(2,1)}, u32[]{:S(2)}) copy-start(bf16[1,1,128,2048]{3,2,1,0:T(8,128)(2,1)} %param.16) | copy-start | bytes 1572868
  192.7 18.4 %copy-start = (bf16[1,1,128,2048]{2,3,1,0:T(8,128)(2,1)S(1)}, bf16[1,1,128,2048]{2,3,1,0:T(8,128)(2,1)}, u32[]{:S(2)}) copy-start(bf16[1,1,128,2048]{2,3,1,0:T(8,128)(2,1)} %copy.34) | copy-start | bytes 1572868
  192.7 30.3 %collective-permute-start.17 = (bf16[128,2048]{1,0:T(8,128)(2,1)}, bf16[128,2048]{1,0:T(8,128)(2,1)}, u32[]{:S(2)}, u32[]{:S(2)}) collective-permute-start(bf16[128,2048]{1,0:T(8,128)(2,1)} %get-tuple-element.33), channel_id=1, source_target_pairs={{1,0},{2,1},{3,2},{4,3},{5,4},{6,5},{7,6},{9,8},{10,9},{11,10},{12... | collective-permute-start | bytes 1572872 | tf_op jit(solution)/shard_map/ppermute | solution.py:17
  194.2 28.9 %collective-permute-start.18 = (bf16[128,2048]{1,0:T(8,128)(2,1)}, bf16[128,2048]{1,0:T(8,128)(2,1)}, u32[]{:S(2)}, u32[]{:S(2)}) collective-permute-start(bf16[128,2048]{1,0:T(8,128)(2,1)} %get-tuple-element.36), channel_id=1, source_target_pairs={{2,0},{3,1},{4,2},{5,3},{6,4},{7,5},{10,8},{11,9},{12,10},{13,11},... | collective-permute-start | bytes 1572872 | tf_op jit(solution)/shard_map/ppermute | solution.py:17
  197.5 25.6 %collective-permute-start.19 = (bf16[128,2048]{1,0:T(8,128)(2,1)}, bf16[128,2048]{1,0:T(8,128)(2,1)}, u32[]{:S(2)}, u32[]{:S(2)}) collective-permute-start(bf16[128,2048]{1,0:T(8,128)(2,1)} %get-tuple-element.35), channel_id=1, source_target_pairs={{3,0},{4,1},{5,2},{6,3},{7,4},{11,8},{12,9},{13,10},{14,11},{15,12... | collective-permute-start | bytes 1572872 | tf_op jit(solution)/shard_map/ppermute | solution.py:17
  201.1 43.3 %collective-permute-start.20 = (bf16[128,2048]{1,0:T(8,128)(2,1)}, bf16[128,2048]{1,0:T(8,128)(2,1)}, u32[]{:S(2)}, u32[]{:S(2)}) collective-permute-start(bf16[128,2048]{1,0:T(8,128)(2,1)} %get-tuple-element.34), channel_id=1, source_target_pairs={{4,0},{5,1},{6,2},{7,3},{12,8},{13,9},{14,10},{15,11},{20,16},{21,... | collective-permute-start | bytes 1572872 | tf_op jit(solution)/shard_map/ppermute | solution.py:17
  223.0 65.7 %collective-permute-start.8 = (bf16[128,2048]{1,0:T(8,128)(2,1)S(1)}, bf16[128,2048]{1,0:T(8,128)(2,1)S(1)}, u32[]{:S(2)}, u32[]{:S(2)}) collective-permute-start(bf16[128,2048]{1,0:T(8,128)(2,1)S(1)} %add_convert_fusion), channel_id=1, source_target_pairs={{0,8},{8,0},{1,9},{9,1},{2,10},{10,2},{3,11},{11,3},{4,12},{12,4},... | collective-permute-start | bytes 1572872 | tf_op jit(solution)/shard_map/ppermute | solution.py:23
  246.5 42.1 %collective-permute-start.21 = (bf16[128,2048]{1,0:T(8,128)(2,1)S(1)}, bf16[128,2048]{1,0:T(8,128)(2,1)S(1)}, u32[]{:S(2)}, u32[]{:S(2)}) collective-permute-start(bf16[128,2048]{1,0:T(8,128)(2,1)S(1)} %fusion.30), channel_id=1, source_target_pairs={{0,8},{8,0},{1,9},{9,1},{2,10},{10,2},{3,11},{11,3},{4,12},{12,4},... | collective-permute-start | bytes 1572872 | tf_op jit(solution)/shard_map/ppermute | solution.py:23
